TPU v7x, 32 devices: a whole 2x2x4 slice. The times are simulated.
32 devices in a mesh: outer: 8 (over z, x), inner: 4 (over y, core).
Axes of the slice: x: 2, y: 2, z: 4, core: 2. Of those that a mesh axis runs over, the one named last changes fastest.
Arguments:
- features: bfloat16 [4096, 4096], P(('outer', 'inner')), may hold values from -6 to 6
- cotangent: bfloat16 [4096, 512], P(('outer', 'inner')), may hold values from -6 to 6
- w_codes: bfloat16 [1024, 4, 512], P('inner'), may hold values from -0.09375 to 0.09375
- w_scales: float32 [1024, 1, 1], P('inner'), may hold values from 0.4 to 2.5
Outputs:
- key_proj: bfloat16 [4096, 512], P(('outer', 'inner'))
- grad_input: bfloat16 [4096, 4096], P(('outer', 'inner'))
- grad_weight: bfloat16 [4096, 512], P(('inner', 'outer'))
All inputs are finite; a program needn't handle non-finite values. Where the computation divides by a largest or mean magnitude, that divisor is 1e-20 or more.
Results may differ from a plain program's by a relative error of at most 0.014.
Values may be sent and summed in bfloat16 or wider, within the bound.
A program may use at most 64 MiB of HBM per device.

v0:
```python
import jax
import jax.numpy as jnp
from jax import lax
from jax.sharding import PartitionSpec as P


def dequantize(codes, scales):
    width = codes.shape[2]
    return (codes.astype(jnp.float32) * scales).astype(jnp.bfloat16).reshape(-1, width)


def forward_part(features, cotangent, w_codes, w_scales):
    all_codes, all_scales = (
        lax.all_gather(w_codes, "inner", axis=0, tiled=True),
        lax.all_gather(w_scales.astype(jnp.bfloat16), "inner", axis=0, tiled=True).astype(
            w_scales.dtype
        ),
    )
    weight = dequantize(all_codes, all_scales)
    key_proj = jnp.dot(features, weight, preferred_element_type=jnp.float32).astype(jnp.bfloat16)
    grad_input = lax.dot_general(
        cotangent, weight, (((1,), (1,)), ((), ())), preferred_element_type=jnp.float32
    ).astype(jnp.bfloat16)
    return (key_proj, grad_input)


def gradient_part(features, cotangent, rows_block):
    width = cotangent.shape[1]
    grad_share = lax.psum_scatter(
        lax.dot_general(
            features, cotangent, (((0,), (0,)), ((), ())), preferred_element_type=jnp.float32
        ).astype(jnp.bfloat16),
        "inner",
        scatter_dimension=0,
        tiled=True,
    ).astype(jnp.float32)
    blocks = grad_share.reshape(-1, rows_block * width)
    block_scale = jnp.max(jnp.abs(blocks), axis=1, keepdims=True) + 1e-06
    block_codes = (blocks / block_scale).astype(jnp.bfloat16).reshape(-1, rows_block, width)
    got_codes, got_scales = (
        lax.all_to_all(block_codes, "outer", split_axis=0, concat_axis=0, tiled=True),
        lax.all_to_all(
            block_scale.reshape(-1, 1, 1).astype(jnp.bfloat16),
            "outer",
            split_axis=0,
            concat_axis=0,
            tiled=True,
        ).astype(jnp.float32),
    )
    senders = lax.axis_size("outer")
    devices = senders * lax.axis_size("inner")
    restored = (got_codes.astype(jnp.float32) * got_scales).reshape(senders, -1, rows_block, width)
    summed = jnp.sum(restored, axis=0).reshape(-1, width)
    return (summed / devices).astype(jnp.bfloat16)


def on_device(features, cotangent, w_codes, w_scales):
    rows_block = w_codes.shape[1]
    key_proj, grad_input = forward_part(features, cotangent, w_codes, w_scales)
    grad_weight = gradient_part(features, cotangent, rows_block)
    return (key_proj, grad_input, grad_weight)


def solution(mesh):
    in_specs = (
        P(("outer", "inner"), None),
        P(("outer", "inner"), None),
        P("inner", None, None),
        P("inner", None, None),
    )
    out_specs = (
        P(("outer", "inner"), None),
        P(("outer", "inner"), None),
        P(("inner", "outer"), None),
    )
    return jax.shard_map(
        on_device, mesh=mesh, in_specs=in_specs, out_specs=out_specs, check_vma=False
    )
```

profile of v0, /device:TPU:0, one launch (start us, length us, event | category | flops | bytes accessed | tf_op | source)
XLA Modules:
  0.0 129.0 jit_solution(7278609064622345255)
XLA Ops:
  7.2 0.0 copy-start
  7.2 0.0 reduce-scatter.2.cloned.1.call-start
  7.2 1.2 copy-done
  8.4 4.1 %convolution_convert_fusion = bf16[4096,512]{1,0:T(8,128)(2,1)} fusion(bf16[128,4096]{1,0:T(8,128)(2,1)S(1)} %copy-done, bf16[128,512]{1,0:T(8,128)(2,1)} %param.5), kind=kOutput, calls=%fused_computation.1 | convolution fusion | flops 538968064 | bytes 5373952 | tf_op jit(solution)/shard_map/dot_general | solution.py:30
  12.5 0.0 reduce-scatter.2.cloned.1.call-update
  12.6 0.0 all-gather.2.cloned.1.call-start
  12.6 0.7 all-gather.2.cloned.1.call-update
  13.3 46.6 %reduce-scatter.2.cloned.1.call-done = bf16[1024,512]{1,0:T(8,128)(2,1)} async-done(((bf16[4096,512]{1,0:T(8,128)(2,1)}), bf16[1024,512]{1,0:T(8,128)(2,1)}) %reduce-scatter.2.cloned.1.call-update) | async-done | bytes 1048592 | tf_op jit(solution)/shard_map/reduce_scatter | solution.py:29
  59.9 1.5 %abs_reduce_fusion = f32[1024]{0:T(1024)S(1)} fusion(bf16[1024,512]{1,0:T(8,128)(2,1)} %reduce-scatter.2.cloned.1.call-done), kind=kLoop, calls=%fused_computation.5 | loop fusion | flops 1571840 | bytes 1052672 | tf_op jit(solution)/shard_map/reduce_max | solution.py:38
  61.5 0.1 reduce_max.14
  61.6 0.1 reduce_max.18
  61.7 1.0 convert_element_type.71
  62.7 5.5 %all-to-all-start.1 = ((bf16[256,1,1]{2,1,0:T(2,128)(2,1)}), bf16[256,1,1]{2,1,0:T(2,128)(2,1)S(1)}, u32[]{:S(2)}, u32[]{:S(2)}) async-start(bf16[256,1,1]{2,1,0:T(2,128)(2,1)} %convert_element_type.71), calls=%async_computation.2 | async-start | bytes 262144 | tf_op jit(solution)/shard_map/all_to_all | solution.py:42
  68.2 1.8 %reshape.48 = f32[256,4,512]{2,1,0:T(4,128)S(1)} reshape(bf16[1024,512]{1,0:T(8,128)(2,1)} %reduce-scatter.2.cloned.1.call-done) | data formatting | bytes 3145728 | tf_op jit(solution)/shard_map/reshape | solution.py:37
  70.0 1.4 %divide_convert_fusion = bf16[256,4,512]{2,1,0:T(4,128)(2,1)} fusion(f32[256,4,512]{2,1,0:T(4,128)S(1)} %reshape.48, f32[256]{0:T(256)S(1)} %get-tuple-element.13), kind=kLoop, calls=%fused_computation.6 | loop fusion | flops 1048576 | bytes 3146752 | tf_op jit(solution)/shard_map/convert_element_type | solution.py:39
  71.5 4.1 %all-to-all-done.1 = bf16[256,1,1]{2,1,0:T(2,128)(2,1)S(1)} async-done(((bf16[256,1,1]{2,1,0:T(2,128)(2,1)}), bf16[256,1,1]{2,1,0:T(2,128)(2,1)S(1)}, u32[]{:S(2)}, u32[]{:S(2)}) %all-to-all-start.1) | async-done | bytes 544 | tf_op jit(solution)/shard_map/all_to_all | solution.py:42
  75.5 4.2 %all-to-all-start = ((bf16[256,4,512]{2,1,0:T(4,128)(2,1)}), bf16[256,4,512]{2,1,0:T(4,128)(2,1)}, u32[]{:S(2)}, u32[]{:S(2)}) async-start(bf16[256,4,512]{2,1,0:T(4,128)(2,1)} %divide_convert_fusion), calls=%async_computation.1 | async-start | bytes 2097152 | tf_op jit(solution)/shard_map/all_to_all | solution.py:41
  79.8 5.1 %all_gather.7 = bf16[1024,1,1]{0,2,1:T(2,128)(2,1)S(1)} all-gather(bf16[256,1,1]{0,2,1:T(2,128)(2,1)S(1)} %convert_element_type.57), channel_id=1, replica_groups=mesh['outer'=8,'inner'=4] {'inner'}, dimensions={0}, use_global_device_ids=true | all-gather | bytes 2560 | tf_op jit(solution)/shard_map/all_gather | solution.py:15
  84.9 11.2 %all-gather.2.cloned.1.call-done = bf16[1024,4,512]{2,1,0:T(4,128)(2,1)} async-done(((bf16[256,4,512]{2,1,0:T(4,128)(2,1)}), bf16[1024,4,512]{2,1,0:T(4,128)(2,1)}) %all-gather.2.cloned.1.call-update) | async-done | bytes 4194320 | tf_op jit(solution)/shard_map/all_gather | solution.py:14
  96.1 6.2 %multiply_convert_fusion = bf16[1024,4,512]{2,1,0:T(4,128)(2,1)} fusion(bf16[1024,4,512]{2,1,0:T(4,128)(2,1)} %all-gather.2.cloned.1.call-done, f32[1024]{0:T(1024)S(1)} %bitcast.13), kind=kLoop, calls=%fused_computation | loop fusion | flops 6291456 | bytes 8392704 | tf_op jit(solution)/shard_map/convert_element_type | solution.py:9
  102.3 7.0 %reshape.47 = bf16[4096,512]{1,0:T(8,128)(2,1)} reshape(bf16[1024,4,512]{2,1,0:T(4,128)(2,1)} %multiply_convert_fusion) | data formatting | bytes 8388608 | tf_op jit(solution)/shard_map/reshape | solution.py:9
  109.3 0.0 copy-done.1
  109.3 3.4 %fusion = bf16[128,4096]{0,1:T(8,128)(2,1)S(1)} fusion(bf16[4096,512]{1,0:T(8,128)(2,1)} %reshape.47, bf16[128,512]{1,0:T(8,128)(2,1)S(1)} %copy-done.1), kind=kOutput, calls=%fused_computation.3 | convolution fusion | flops 537395200 | bytes 5373952 | tf_op jit(solution)/shard_map/dot_general | solution.py:21
  112.7 1.3 %copy.13 = bf16[128,4096]{1,0:T(8,128)(2,1)} copy(bf16[128,4096]{0,1:T(8,128)(2,1)S(1)} %fusion) | data formatting | bytes 2097152
  114.0 3.5 %fusion.1 = bf16[128,512]{0,1:T(8,128)(2,1)S(1)} fusion(bf16[4096,512]{1,0:T(8,128)(2,1)} %reshape.47, bf16[128,4096]{1,0:T(8,128)(2,1)S(1)} %copy-done), kind=kOutput, calls=%fused_computation.8 | convolution fusion | flops 536936448 | bytes 5373952 | tf_op jit(solution)/shard_map/dot_general | solution.py:20
  117.5 0.8 copy.12
  118.3 1.0 convert_reduce_fusion
  119.3 0.0 all-to-all-done
  119.3 1.7 %convert_multiply_fusion = f32[256,4,512]{2,1,0:T(4,128)S(1)} fusion(bf16[256,4,512]{2,1,0:T(4,128)(2,1)} %all-to-all-done, f32[256]{0:T(256)S(1)} %convert_reduce_fusion), kind=kLoop, calls=%fused_computation.4 | loop fusion | flops 1048576 | bytes 3146752 | tf_op jit(solution)/shard_map/mul | solution.py:52
  121.0 0.4 reduce_sum.9
  121.4 0.1 multiply_convert_fusion.1
  121.5 0.7 convert_element_type.70
  (6 shorter events, 0.0 us)
Async XLA Ops:
  7.2 1.2 copy-start
  7.2 52.8 %reduce-scatter.2.cloned.1.call-start = ((), (), s32[]{:S(2)}) async-start(), calls=%async_computation.4 | async-start | bytes 5242880 | tf_op jit(solution)/shard_map/reduce_scatter | solution.py:29
  12.6 83.5 %all-gather.2.cloned.1.call-start = ((), (), s32[]{:S(2)}) async-start(), calls=%async_computation.3 | async-start | bytes 5242880 | tf_op jit(solution)/shard_map/all_gather | solution.py:14
  62.7 12.8 %all-to-all-start.1 = ((bf16[256,1,1]{2,1,0:T(2,128)(2,1)}), bf16[256,1,1]{2,1,0:T(2,128)(2,1)S(1)}, u32[]{:S(2)}, u32[]{:S(2)}) async-start(bf16[256,1,1]{2,1,0:T(2,128)(2,1)} %convert_element_type.71), calls=%async_computation.2 | async-start | bytes 262144 | tf_op jit(solution)/shard_map/all_to_all | solution.py:42
  68.2 11.6 %copy-start.2 = (f32[256,1,1]{0,2,1:T(1,128)S(1)}, f32[256,1,1]{0,2,1:T(1,128)}, u32[]{:S(2)}) copy-start(f32[256,1,1]{0,2,1:T(1,128)} %param.7) | copy-start | bytes 3076
  75.5 43.8 %all-to-all-start = ((bf16[256,4,512]{2,1,0:T(4,128)(2,1)}), bf16[256,4,512]{2,1,0:T(4,128)(2,1)}, u32[]{:S(2)}, u32[]{:S(2)}) async-start(bf16[256,4,512]{2,1,0:T(4,128)(2,1)} %divide_convert_fusion), calls=%async_computation.1 | async-start | bytes 2097152 | tf_op jit(solution)/shard_map/all_to_all | solution.py:41
  102.3 7.0 %copy-start.1 = (bf16[128,512]{1,0:T(8,128)(2,1)S(1)}, bf16[128,512]{1,0:T(8,128)(2,1)}, u32[]{:S(2)}) copy-start(bf16[128,512]{1,0:T(8,128)(2,1)} %param.5) | copy-start | bytes 393220
Sparse Core Ops, SparseCore 0:
  12.7 47.2 reduce-scatter.1
  61.6 34.4 all-gather.1
where the time goes:
time: 130 us; the launch traced here: 129 us
  waiting for transfers between devices  62.6 us (48%)
  between operations  14.1 us (11%)
  local copies, waits for them, and re-layouts  13.9 us (11%)
  other arithmetic  12.4 us (10%)
  matrix products  11.1 us (9%)
  starting transfers between devices  9.82 us (8%)
  blocking collectives  5.07 us (4%)
    reduce_scatter x1, waiting for transfers between devices, gradient_part(): lax.psum_scatter(lax.dot_general(features, cotangent, (((0,), (0,)), ((),...  46.6 us
    all_gather x1, waiting for transfers between devices, forward_part(): lax.all_gather(w_codes, 'inner', axis=0, tiled=True)  11.2 us
    reshape x1, local copies, waits for them, and re-layouts, dequantize(): (codes.astype(jnp.float32) * scales).astype(jnp.bfloat16).reshape(-1, width)  6.96 us
    convert_element_type x1, other arithmetic, dequantize(): (codes.astype(jnp.float32) * scales).astype(jnp.bfloat16).reshape(-1, width)  6.2 us
    all_to_all x1, starting transfers between devices, gradient_part(): lax.all_to_all(block_scale.reshape(-1, 1, 1).astype(jnp.bfloat16), 'outer...  5.49 us
    all_gather x1, blocking collectives, forward_part(): lax.all_gather(w_scales.astype(jnp.bfloat16), 'inner', axis=0, tiled=True)  5.07 us
    all_to_all x1, starting transfers between devices, gradient_part(): lax.all_to_all(block_codes, 'outer', split_axis=0, concat_axis=0, tiled=T...  4.25 us
    dot_general x1, matrix products, gradient_part(): lax.dot_general(features, cotangent, (((0,), (0,)), ((), ())), preferred_...  4.15 us
  transfers between devices with their start and end apart: 4, of which 3 were waited for; matrix products, arithmetic and copies ran while one was open for 23% of the time, Pallas kernels for 0%

commit v1 on v0

--- a/solution.py
+++ b/solution.py
@@ -1,6 +1,10 @@
+import functools
+
 import jax
 import jax.numpy as jnp
 from jax import lax
+from jax.experimental import pallas as pl
+from jax.experimental.pallas import tpu as pltpu
 from jax.sharding import PartitionSpec as P
 
 
@@ -10,13 +14,7 @@
 
 
 def forward_part(features, cotangent, w_codes, w_scales):
-    all_codes, all_scales = (
-        lax.all_gather(w_codes, "inner", axis=0, tiled=True),
-        lax.all_gather(w_scales.astype(jnp.bfloat16), "inner", axis=0, tiled=True).astype(
-            w_scales.dtype
-        ),
-    )
-    weight = dequantize(all_codes, all_scales)
+    weight = lax.all_gather(dequantize(w_codes, w_scales), "inner", axis=0, tiled=True)
     key_proj = jnp.dot(features, weight, preferred_element_type=jnp.float32).astype(jnp.bfloat16)
     grad_input = lax.dot_general(
         cotangent, weight, (((1,), (1,)), ((), ())), preferred_element_type=jnp.float32
@@ -61,6 +59,194 @@
     return (key_proj, grad_input, grad_weight)
 
 
+WEIGHT_OF = {"y": 16, "core": 8, "zh": 4, "zl": 2, "x": 1}
+STREAMS = (("core", "x", "y", "zl", "zh"), ("core", "zl", "y", "x", "zh"))
+MESH = pl.DeviceIdType.MESH
+
+
+def kernel(feat, cot, own, key_ref, gin_ref, gw_ref, part, got, held, acc, w_send, w_recv, g_send, g_recv):
+    outer, inner = lax.axis_index("outer"), lax.axis_index("inner")
+    bit = {
+        "x": outer % 2,
+        "zl": (outer // 2) % 2,
+        "zh": outer // 4,
+        "core": inner % 2,
+        "y": inner // 2,
+    }
+
+    def flip(v, b, step):
+        return v + step - 2 * step * b
+
+    partner = {
+        "x": (flip(outer, bit["x"], 1), inner),
+        "zl": (flip(outer, bit["zl"], 2), inner),
+        "zh": (flip(outer, bit["zh"], 4), inner),
+        "core": (outer, flip(inner, bit["core"], 1)),
+        "y": (outer, flip(inner, bit["y"], 2)),
+    }
+    barrier = pltpu.get_barrier_semaphore()
+    for p in partner.values():
+        pl.semaphore_signal(barrier, inc=1, device_id=p, device_id_type=MESH)
+    pl.semaphore_wait(barrier, len(partner))
+
+    rows = part.shape[2]
+    cols = part.shape[3]
+    half = own.shape[1]
+    mine = bit["x"]
+    other = 1 - mine
+
+    def remote(src, dst, send, recv, dim):
+        return pltpu.make_async_remote_copy(
+            src_ref=src, dst_ref=dst, send_sem=send, recv_sem=recv,
+            device_id=partner[dim], device_id_type=MESH,
+        )
+
+    def w_copy(n, src, dst, dim):
+        return remote(src, dst, w_send.at[n], w_recv.at[n], dim)
+
+    def g_copy(s, step):
+        n = 16 >> step
+        return remote(
+            part.at[s, pl.ds(n, n)], got.at[s, pl.ds(n, n)],
+            g_send.at[s, step], g_recv.at[s, step], STREAMS[s][step],
+        )
+
+    over_y = w_copy(0, own.at[mine], held.at[1, mine], "y")
+    over_core = w_copy(1, own, held.at[0], "core")
+    over_x = w_copy(2, held.at[1, mine], held.at[1, mine], "x")
+    core_mine = w_copy(3, held.at[1, mine], held.at[2, mine], "core")
+    core_other = w_copy(4, held.at[1, other], held.at[2, other], "core")
+    g = [[g_copy(s, step) for step in range(5)] for s in range(2)]
+
+    over_y.start()
+
+    def partial(n):
+        rel, rest = {}, n
+        for dim in reversed(STREAMS[0]):
+            rel[dim] = rest % 2
+            rest = rest // 2
+        block = 0
+        for dim, w in WEIGHT_OF.items():
+            block = block + w * (rel[dim] + bit[dim] - 2 * rel[dim] * bit[dim])
+        second = 0
+        for dim in STREAMS[1]:
+            second = second * 2 + rel[dim]
+        at = pl.multiple_of(block * rows, rows)
+        value = lax.dot_general(
+            feat[:, pl.ds(at, rows)], cot[...], (((0,), (0,)), ((), ())),
+            preferred_element_type=jnp.float32,
+        ).astype(jnp.bfloat16)
+        part[0, n] = value[:, :cols]
+        part[1, second] = value[:, cols:]
+
+    for n in range(16, 32):
+        partial(n)
+    g[0][0].start()
+    g[1][0].start()
+    over_core.start()
+    for n in range(16):
+        partial(n)
+
+    def add(s, lo, n, base):
+        @pl.loop(lo, lo + n)
+        def _(j):
+            part[s, j] = (
+                part[s, j].astype(jnp.float32) + got[s, base + j].astype(jnp.float32)
+            ).astype(jnp.bfloat16)
+
+    def advance(s, step):
+        n = 16 >> step
+        g[s][step].wait_recv()
+        add(s, n // 2, n // 2, n)
+        g[s][step + 1].start()
+        add(s, 0, n // 2, n)
+
+    def finish(s):
+        g[s][4].wait_recv()
+        total = part[s, 0].astype(jnp.float32) + got[s, 1].astype(jnp.float32)
+        devices = lax.axis_size("outer") * lax.axis_size("inner")
+        gw_ref[:, s * cols:(s + 1) * cols] = (total / devices).astype(jnp.bfloat16)
+
+    flipped_core = flip(inner, bit["core"], 1)
+    flipped_y = flip(inner, bit["y"], 2)
+    flipped_both = flip(flipped_core, bit["y"], 2)
+
+    def unit(block, shard, h, first=False):
+        at = pl.multiple_of((shard * 2 + h) * half, half)
+        value = jnp.dot(feat[:, pl.ds(at, half)], block[...], preferred_element_type=jnp.float32)
+        acc[...] = value if first else acc[...] + value
+        gin_ref[:, pl.ds(at, half)] = lax.dot_general(
+            cot[...], block[...], (((1,), (1,)), ((), ())), preferred_element_type=jnp.float32
+        ).astype(jnp.bfloat16)
+
+    advance(0, 0)
+    advance(1, 0)
+    unit(own.at[0], inner, 0, first=True)
+    unit(own.at[1], inner, 1)
+    over_core.wait_recv()
+    unit(held.at[0, 0], flipped_core, 0)
+    unit(held.at[0, 1], flipped_core, 1)
+    over_y.wait_recv()
+    over_x.start()
+    core_mine.start()
+    unit(held.at[1, mine], flipped_y, mine)
+    advance(0, 1)
+    advance(1, 1)
+    core_mine.wait_recv()
+    unit(held.at[2, mine], flipped_both, mine)
+    advance(0, 2)
+    advance(1, 2)
+    over_x.wait_recv()
+    core_other.start()
+    advance(0, 3)
+    advance(1, 3)
+    unit(held.at[1, other], flipped_y, other)
+    core_other.wait_recv()
+    unit(held.at[2, other], flipped_both, other)
+    key_ref[...] = acc[...].astype(jnp.bfloat16)
+    finish(0)
+    finish(1)
+    for copy in (over_y, over_core, over_x, core_mine, core_other, *g[0], *g[1]):
+        copy.wait_send()
+
+
+def fused(features, cotangent, w_codes, w_scales):
+    tokens, depth = features.shape
+    width = cotangent.shape[1]
+    weight = dequantize(w_codes, w_scales)
+    half = weight.shape[0] // 2
+    rows = depth // 32
+    cols = width // 2
+    bf16 = jnp.bfloat16
+    vmem = pl.BlockSpec(memory_space=pltpu.VMEM)
+    return pl.pallas_call(
+        kernel,
+        out_shape=(
+            jax.ShapeDtypeStruct((tokens, width), bf16),
+            jax.ShapeDtypeStruct((tokens, depth), bf16),
+            jax.ShapeDtypeStruct((rows, width), bf16),
+        ),
+        in_specs=[vmem] * 3,
+        out_specs=(vmem,) * 3,
+        scratch_shapes=[
+            pltpu.VMEM((2, 32, rows, cols), bf16),
+            pltpu.VMEM((2, 32, rows, cols), bf16),
+            pltpu.VMEM((3, 2, half, width), bf16),
+            pltpu.VMEM((tokens, width), jnp.float32),
+            pltpu.SemaphoreType.DMA((5,)),
+            pltpu.SemaphoreType.DMA((5,)),
+            pltpu.SemaphoreType.DMA((2, 5)),
+            pltpu.SemaphoreType.DMA((2, 5)),
+        ],
+        compiler_params=pltpu.CompilerParams(
+            collective_id=0, has_side_effects=True, vmem_limit_bytes=40 * 1024 * 1024
+        ),
+        cost_estimate=pl.CostEstimate(
+            flops=6 * tokens * depth * width, bytes_accessed=8 * tokens * depth, transcendentals=0
+        ),
+    )(features, cotangent, weight.reshape(2, half, width))
+
+
 def solution(mesh):
     in_specs = (
         P(("outer", "inner"), None),
@@ -73,6 +259,8 @@
         P(("outer", "inner"), None),
         P(("inner", "outer"), None),
     )
+    small = mesh.shape["outer"] == 8 and mesh.shape["inner"] == 4
     return jax.shard_map(
-        on_device, mesh=mesh, in_specs=in_specs, out_specs=out_specs, check_vma=False
-    )
+        fused if small else on_device,
+        mesh=mesh, in_specs=in_specs, out_specs=out_specs, check_vma=False,
+    )

time: 130 us -> 50.6 us (0.39)
  waiting for transfers between devices: 62.6 us -> 0 us
  Pallas kernels: 0 us -> 44.6 us
  between operations: 14.1 us -> 0.67 us
  matrix products: 11.1 us -> 0 us
  other arithmetic: 12.4 us -> 1.7 us
  local copies, waits for them, and re-layouts: 13.9 us -> 3.49 us
  starting transfers between devices: 9.82 us -> 0 us
  blocking collectives: 5.07 us -> 0 us
    reduce_scatter x1 -> x0, waiting for transfers between devices: 46.6 us -> none  [gradient_part(): lax.psum_scatter(lax.dot_general(features, cotangent, (((0,), (0,)), ((),...]
    pallas_call x0 -> x1, Pallas kernels: none -> 44.6 us  [fused(): pl.pallas_call(kernel, out_shape=(jax.ShapeDtypeStruct((tokens, width), b...]
    all_gather x1 -> x0, waiting for transfers between devices: 11.2 us -> none  [forward_part(): lax.all_gather(w_codes, 'inner', axis=0, tiled=True)]
    dot_general x3 -> x0, matrix products: 11.1 us -> none  [the longest x1 4.15 us: gradient_part(): lax.dot_general(features, cotangent, (((0,), (0,)), ((), ())), preferred_...]
    all_to_all x2 -> x0, starting transfers between devices: 9.74 us -> none  [the longest x1 5.49 us: gradient_part(): lax.all_to_all(block_scale.reshape(-1, 1, 1).astype(jnp.bfloat16), 'outer...]
    reshape x2 -> x0, local copies, waits for them, and re-layouts: 8.77 us -> none  [the longest x1 6.96 us: dequantize(): (codes.astype(jnp.float32) * scales).astype(jnp.bfloat16).reshape(-1, width)]
    all_gather x1 -> x0, blocking collectives: 5.07 us -> none  [forward_part(): lax.all_gather(w_scales.astype(jnp.bfloat16), 'inner', axis=0, tiled=True)]
    convert_element_type x1, other arithmetic: 6.2 us -> 1.7 us  [dequantize(): (codes.astype(jnp.float32) * scales).astype(jnp.bfloat16).reshape(-1, width)]
  transfers between devices with their start and end apart: 4 -> 0, of which waited for: 3 -> 0; matrix products, arithmetic and copies ran while one was open for 23% -> 0% of each run, Pallas kernels for 0% -> 0%
where the time goes in v1:
time: 50.6 us; the launch traced here: 50.4 us
  Pallas kernels  44.6 us (88%)
  local copies, waits for them, and re-layouts  3.49 us (7%)
  other arithmetic  1.7 us (3%)
  between operations  0.67 us (1%)
    pallas_call x1, Pallas kernels, fused(): pl.pallas_call(kernel, out_shape=(jax.ShapeDtypeStruct((tokens, width), b...  44.6 us
    unnamed x7, local copies, waits for them, and re-layouts  3.2 us
    convert_element_type x1, other arithmetic, dequantize(): (codes.astype(jnp.float32) * scales).astype(jnp.bfloat16).reshape(-1, width)  1.7 us

profile of v1, /device:TPU:0, one launch (start us, length us, event | category | flops | bytes accessed | tf_op | source)
XLA Modules:
  0.0 50.4 jit_solution(5892187885779565422)
XLA Ops:
  0.6 1.7 %multiply_convert_fusion = bf16[256,4,512]{2,1,0:T(4,128)(2,1)S(1)} fusion(bf16[256,4,512]{2,1,0:T(4,128)(2,1)} %param.6, f32[256]{0:T(256)} %bitcast.1), kind=kLoop, calls=%fused_computation | loop fusion | flops 1572864 | bytes 2098176 | tf_op jit(solution)/shard_map/convert_element_type | solution.py:13
  2.3 0.0 copy-start
  2.3 0.0 copy-start.1
  2.4 0.3 reshape_reshape.3.own
  2.7 0.9 %copy-done = bf16[128,4096]{1,0:T(8,128)(2,1)S(1)} copy-done((bf16[128,4096]{1,0:T(8,128)(2,1)S(1)}, bf16[128,4096]{1,0:T(8,128)(2,1)}, u32[]{:S(2)}) %copy-start) | copy-done | bytes 1048600
  3.6 0.0 copy-done.1
  3.6 44.6 %shard_map.67 = (bf16[128,512]{1,0:T(8,128)(2,1)S(1)}, bf16[128,4096]{1,0:T(8,128)(2,1)S(1)}, bf16[128,512]{1,0:T(8,128)(2,1)S(1)}) custom-call(bf16[128,4096]{1,0:T(8,128)(2,1)S(1)} %copy-done, bf16[128,512]{1,0:T(8,128)(2,1)S(1)} %copy-done.1, bf16[2,512,512]{2,1,0:T(8,128)(2,1)S(1)} %reshape_reshape.3.own), custom_call_target="tpu_custom_call" | custom-call | flops 1610612736 | bytes 4194304 | tf_op jit(solution)/shard_map/pallas_call | solution.py:222
  48.2 0.7 %copy.10 = bf16[128,512]{1,0:T(8,128)(2,1)} copy(bf16[128,512]{1,0:T(8,128)(2,1)S(1)} %get-tuple-element.6) | data formatting | bytes 262144
  48.8 1.0 %copy.11 = bf16[128,4096]{1,0:T(8,128)(2,1)} copy(bf16[128,4096]{1,0:T(8,128)(2,1)S(1)} %get-tuple-element.7) | data formatting | bytes 2097152
  49.8 0.7 %copy.12 = bf16[128,512]{1,0:T(8,128)(2,1)} copy(bf16[128,512]{1,0:T(8,128)(2,1)S(1)} %get-tuple-element.8) | data formatting | bytes 262144
Async XLA Ops:
  2.3 1.2 %copy-start = (bf16[128,4096]{1,0:T(8,128)(2,1)S(1)}, bf16[128,4096]{1,0:T(8,128)(2,1)}, u32[]{:S(2)}) copy-start(bf16[128,4096]{1,0:T(8,128)(2,1)} %feat.1) | copy-start | bytes 3145732
  2.3 1.2 %copy-start.1 = (bf16[128,512]{1,0:T(8,128)(2,1)S(1)}, bf16[128,512]{1,0:T(8,128)(2,1)}, u32[]{:S(2)}) copy-start(bf16[128,512]{1,0:T(8,128)(2,1)} %cot.1) | copy-start | bytes 393220

commit v2 on v1

--- a/solution.py
+++ b/solution.py
@@ -60,7 +60,12 @@
 
 
 WEIGHT_OF = {"y": 16, "core": 8, "zh": 4, "zl": 2, "x": 1}
-STREAMS = (("core", "x", "y", "zl", "zh"), ("core", "zl", "y", "x", "zh"))
+STREAMS = (
+    ("core", "x", "y", "zl", "zh"),
+    ("core", "zl", "y", "x", "zh"),
+    ("core", "x", "zl", "y", "zh"),
+    ("core", "zl", "x", "y", "zh"),
+)
 MESH = pl.DeviceIdType.MESH
 
 
@@ -104,11 +109,10 @@
     def w_copy(n, src, dst, dim):
         return remote(src, dst, w_send.at[n], w_recv.at[n], dim)
 
-    def g_copy(s, step):
-        n = 16 >> step
+    def g_copy(s, sem, step, at, n):
         return remote(
-            part.at[s, pl.ds(n, n)], got.at[s, pl.ds(n, n)],
-            g_send.at[s, step], g_recv.at[s, step], STREAMS[s][step],
+            part.at[s, pl.ds(at, n)], got.at[s, pl.ds(at, n)],
+            g_send.at[s, sem], g_recv.at[s, sem], STREAMS[s][step],
         )
 
     over_y = w_copy(0, own.at[mine], held.at[1, mine], "y")
@@ -116,7 +120,12 @@
     over_x = w_copy(2, held.at[1, mine], held.at[1, mine], "x")
     core_mine = w_copy(3, held.at[1, mine], held.at[2, mine], "core")
     core_other = w_copy(4, held.at[1, other], held.at[2, other], "core")
-    g = [[g_copy(s, step) for step in range(5)] for s in range(2)]
+    streams = range(len(STREAMS))
+    first = [g_copy(s, 5, 0, 24, 8) for s in streams]
+    g = [
+        [g_copy(s, step, step, 16 >> step, 8 if step == 0 else 16 >> step) for step in range(5)]
+        for s in streams
+    ]
 
     over_y.start()
 
@@ -128,21 +137,29 @@
         block = 0
         for dim, w in WEIGHT_OF.items():
             block = block + w * (rel[dim] + bit[dim] - 2 * rel[dim] * bit[dim])
-        second = 0
-        for dim in STREAMS[1]:
-            second = second * 2 + rel[dim]
         at = pl.multiple_of(block * rows, rows)
         value = lax.dot_general(
             feat[:, pl.ds(at, rows)], cot[...], (((0,), (0,)), ((), ())),
             preferred_element_type=jnp.float32,
         ).astype(jnp.bfloat16)
-        part[0, n] = value[:, :cols]
-        part[1, second] = value[:, cols:]
-
-    for n in range(16, 32):
-        partial(n)
-    g[0][0].start()
-    g[1][0].start()
+        for s, order in enumerate(STREAMS):
+            place = 0
+            for dim in order:
+                place = place * 2 + rel[dim]
+            part[s, place] = value[:, s * cols:(s + 1) * cols]
+
+    for n in range(24, 32):
+        partial(n)
+    first[0].start()
+    first[2].start()
+    for n in (18, 19, 22, 23):
+        partial(n)
+    first[1].start()
+    first[3].start()
+    for n in (16, 17, 20, 21):
+        partial(n)
+    for s in streams:
+        g[s][0].start()
     over_core.start()
     for n in range(16):
         partial(n)
@@ -156,9 +173,11 @@
 
     def advance(s, step):
         n = 16 >> step
-        g[s][step].wait_recv()
+        (first[s] if step == 0 else g[s][step]).wait_recv()
         add(s, n // 2, n // 2, n)
         g[s][step + 1].start()
+        if step == 0:
+            g[s][0].wait_recv()
         add(s, 0, n // 2, n)
 
     def finish(s):
@@ -179,8 +198,11 @@
             cot[...], block[...], (((1,), (1,)), ((), ())), preferred_element_type=jnp.float32
         ).astype(jnp.bfloat16)
 
-    advance(0, 0)
-    advance(1, 0)
+    def advance_all(step):
+        for s in streams:
+            advance(s, step)
+
+    advance_all(0)
     unit(own.at[0], inner, 0, first=True)
     unit(own.at[1], inner, 1)
     over_core.wait_recv()
@@ -190,23 +212,20 @@
     over_x.start()
     core_mine.start()
     unit(held.at[1, mine], flipped_y, mine)
-    advance(0, 1)
-    advance(1, 1)
+    advance_all(1)
     core_mine.wait_recv()
     unit(held.at[2, mine], flipped_both, mine)
-    advance(0, 2)
-    advance(1, 2)
+    advance_all(2)
     over_x.wait_recv()
     core_other.start()
-    advance(0, 3)
-    advance(1, 3)
+    advance_all(3)
     unit(held.at[1, other], flipped_y, other)
     core_other.wait_recv()
     unit(held.at[2, other], flipped_both, other)
     key_ref[...] = acc[...].astype(jnp.bfloat16)
-    finish(0)
-    finish(1)
-    for copy in (over_y, over_core, over_x, core_mine, core_other, *g[0], *g[1]):
+    for s in streams:
+        finish(s)
+    for copy in (over_y, over_core, over_x, core_mine, core_other, *first, *sum(g, [])):
         copy.wait_send()
 
 
@@ -216,7 +235,7 @@
     weight = dequantize(w_codes, w_scales)
     half = weight.shape[0] // 2
     rows = depth // 32
-    cols = width // 2
+    cols = width // len(STREAMS)
     bf16 = jnp.bfloat16
     vmem = pl.BlockSpec(memory_space=pltpu.VMEM)
     return pl.pallas_call(
@@ -229,14 +248,14 @@
         in_specs=[vmem] * 3,
         out_specs=(vmem,) * 3,
         scratch_shapes=[
-            pltpu.VMEM((2, 32, rows, cols), bf16),
-            pltpu.VMEM((2, 32, rows, cols), bf16),
+            pltpu.VMEM((len(STREAMS), 32, rows, cols), bf16),
+            pltpu.VMEM((len(STREAMS), 32, rows, cols), bf16),
             pltpu.VMEM((3, 2, half, width), bf16),
             pltpu.VMEM((tokens, width), jnp.float32),
             pltpu.SemaphoreType.DMA((5,)),
             pltpu.SemaphoreType.DMA((5,)),
-            pltpu.SemaphoreType.DMA((2, 5)),
-            pltpu.SemaphoreType.DMA((2, 5)),
+            pltpu.SemaphoreType.DMA((len(STREAMS), 6)),
+            pltpu.SemaphoreType.DMA((len(STREAMS), 6)),
         ],
         compiler_params=pltpu.CompilerParams(
             collective_id=0, has_side_effects=True, vmem_limit_bytes=40 * 1024 * 1024

time: 50.6 us -> 48.7 us (0.962)
  Pallas kernels: 44.6 us -> 42.7 us
    pallas_call x1, Pallas kernels: 44.6 us -> 42.7 us  [fused(): pl.pallas_call(kernel, out_shape=(jax.ShapeDtypeStruct((tokens, width), b...]
where the time goes in v2:
time: 48.7 us; the launch traced here: 48.5 us
  Pallas kernels  42.7 us (88%)
  local copies, waits for them, and re-layouts  3.49 us (7%)
  other arithmetic  1.7 us (3%)
  between operations  0.67 us (1%)
    pallas_call x1, Pallas kernels, fused(): pl.pallas_call(kernel, out_shape=(jax.ShapeDtypeStruct((tokens, width), b...  42.7 us
    unnamed x7, local copies, waits for them, and re-layouts  3.2 us
    convert_element_type x1, other arithmetic, dequantize(): (codes.astype(jnp.float32) * scales).astype(jnp.bfloat16).reshape(-1, width)  1.7 us

profile of v2, /device:TPU:0, one launch (start us, length us, event | category | flops | bytes accessed | tf_op | source)
XLA Modules:
  0.0 48.5 jit_solution(10199991117649298650)
XLA Ops:
  0.6 1.7 %multiply_convert_fusion = bf16[256,4,512]{2,1,0:T(4,128)(2,1)S(1)} fusion(bf16[256,4,512]{2,1,0:T(4,128)(2,1)} %param.6, f32[256]{0:T(256)} %bitcast.1), kind=kLoop, calls=%fused_computation | loop fusion | flops 1572864 | bytes 2098176 | tf_op jit(solution)/shard_map/convert_element_type | solution.py:13
  2.3 0.0 copy-start
  2.3 0.0 copy-start.1
  2.4 0.3 reshape_reshape.3.own
  2.7 0.9 %copy-done = bf16[128,4096]{1,0:T(8,128)(2,1)S(1)} copy-done((bf16[128,4096]{1,0:T(8,128)(2,1)S(1)}, bf16[128,4096]{1,0:T(8,128)(2,1)}, u32[]{:S(2)}) %copy-start) | copy-done | bytes 1048600
  3.6 0.0 copy-done.1
  3.6 42.7 %shard_map.67 = (bf16[128,512]{1,0:T(8,128)(2,1)S(1)}, bf16[128,4096]{1,0:T(8,128)(2,1)S(1)}, bf16[128,512]{1,0:T(8,128)(2,1)S(1)}) custom-call(bf16[128,4096]{1,0:T(8,128)(2,1)S(1)} %copy-done, bf16[128,512]{1,0:T(8,128)(2,1)S(1)} %copy-done.1, bf16[2,512,512]{2,1,0:T(8,128)(2,1)S(1)} %reshape_reshape.3.own), custom_call_target="tpu_custom_call" | custom-call | flops 1610612736 | bytes 4194304 | tf_op jit(solution)/shard_map/pallas_call | solution.py:241
  46.3 0.7 %copy.10 = bf16[128,512]{1,0:T(8,128)(2,1)} copy(bf16[128,512]{1,0:T(8,128)(2,1)S(1)} %get-tuple-element.6) | data formatting | bytes 262144
  46.9 1.0 %copy.11 = bf16[128,4096]{1,0:T(8,128)(2,1)} copy(bf16[128,4096]{1,0:T(8,128)(2,1)S(1)} %get-tuple-element.7) | data formatting | bytes 2097152
  47.9 0.7 %copy.12 = bf16[128,512]{1,0:T(8,128)(2,1)} copy(bf16[128,512]{1,0:T(8,128)(2,1)S(1)} %get-tuple-element.8) | data formatting | bytes 262144
Async XLA Ops:
  2.3 1.2 %copy-start = (bf16[128,4096]{1,0:T(8,128)(2,1)S(1)}, bf16[128,4096]{1,0:T(8,128)(2,1)}, u32[]{:S(2)}) copy-start(bf16[128,4096]{1,0:T(8,128)(2,1)} %feat.1) | copy-start | bytes 3145732
  2.3 1.2 %copy-start.1 = (bf16[128,512]{1,0:T(8,128)(2,1)S(1)}, bf16[128,512]{1,0:T(8,128)(2,1)}, u32[]{:S(2)}) copy-start(bf16[128,512]{1,0:T(8,128)(2,1)} %cot.1) | copy-start | bytes 393220

commit v3 on v2

--- a/solution.py
+++ b/solution.py
@@ -66,6 +66,7 @@
     ("core", "x", "zl", "y", "zh"),
     ("core", "zl", "x", "y", "zh"),
 )
+CHUNKS = 4
 MESH = pl.DeviceIdType.MESH
 
 
@@ -97,7 +98,7 @@
     rows = part.shape[2]
     cols = part.shape[3]
     half = own.shape[1]
-    mine = bit["x"]
+    mine = bit["x"] + bit["zl"] - 2 * bit["x"] * bit["zl"]
     other = 1 - mine
 
     def remote(src, dst, send, recv, dim):
@@ -115,11 +116,25 @@
             g_send.at[s, sem], g_recv.at[s, sem], STREAMS[s][step],
         )
 
-    over_y = w_copy(0, own.at[mine], held.at[1, mine], "y")
-    over_core = w_copy(1, own, held.at[0], "core")
-    over_x = w_copy(2, held.at[1, mine], held.at[1, mine], "x")
-    core_mine = w_copy(3, held.at[1, mine], held.at[2, mine], "core")
-    core_other = w_copy(4, held.at[1, other], held.at[2, other], "core")
+    def chunk(ref, h, c):
+        return ref.at[h, pl.ds(c * (half // CHUNKS), half // CHUNKS)]
+
+    chunks = range(CHUNKS)
+    over_core = w_copy(4 * CHUNKS, own, held.at[0], "core")
+    over_y = [w_copy(c, chunk(own, mine, c), chunk(held.at[1], mine, c), "y") for c in chunks]
+    onward = [
+        w_copy(
+            CHUNKS + c, chunk(held.at[1], mine, c), chunk(held.at[1], mine, c), ("x", "zl")[c % 2]
+        )
+        for c in chunks
+    ]
+    core_mine, core_other = [
+        [
+            w_copy((2 + k) * CHUNKS + c, chunk(held.at[1], h, c), chunk(held.at[2], h, c), "core")
+            for c in chunks
+        ]
+        for k, h in enumerate((mine, other))
+    ]
     streams = range(len(STREAMS))
     first = [g_copy(s, 5, 0, 24, 8) for s in streams]
     g = [
@@ -127,7 +142,17 @@
         for s in streams
     ]
 
-    over_y.start()
+    for c in chunks:
+        over_y[c].start()
+
+    def forward(c):
+        over_y[c].wait_recv()
+        onward[c].start()
+        core_mine[c].start()
+
+    def across(c):
+        onward[c].wait_recv()
+        core_other[c].start()
 
     def partial(n):
         rel, rest = {}, n
@@ -202,30 +227,35 @@
         for s in streams:
             advance(s, step)
 
+    forward(0)
     advance_all(0)
+    forward(1)
     unit(own.at[0], inner, 0, first=True)
     unit(own.at[1], inner, 1)
     over_core.wait_recv()
     unit(held.at[0, 0], flipped_core, 0)
     unit(held.at[0, 1], flipped_core, 1)
-    over_y.wait_recv()
-    over_x.start()
-    core_mine.start()
+    for c in range(2, CHUNKS):
+        forward(c)
     unit(held.at[1, mine], flipped_y, mine)
     advance_all(1)
-    core_mine.wait_recv()
+    for c in chunks:
+        core_mine[c].wait_recv()
     unit(held.at[2, mine], flipped_both, mine)
+    across(0)
+    across(1)
     advance_all(2)
-    over_x.wait_recv()
-    core_other.start()
+    for c in range(2, CHUNKS):
+        across(c)
     advance_all(3)
     unit(held.at[1, other], flipped_y, other)
-    core_other.wait_recv()
+    for c in chunks:
+        core_other[c].wait_recv()
     unit(held.at[2, other], flipped_both, other)
     key_ref[...] = acc[...].astype(jnp.bfloat16)
     for s in streams:
         finish(s)
-    for copy in (over_y, over_core, over_x, core_mine, core_other, *first, *sum(g, [])):
+    for copy in (over_core, *over_y, *onward, *core_mine, *core_other, *first, *sum(g, [])):
         copy.wait_send()
 
 
@@ -252,8 +282,8 @@
             pltpu.VMEM((len(STREAMS), 32, rows, cols), bf16),
             pltpu.VMEM((3, 2, half, width), bf16),
             pltpu.VMEM((tokens, width), jnp.float32),
-            pltpu.SemaphoreType.DMA((5,)),
-            pltpu.SemaphoreType.DMA((5,)),
+            pltpu.SemaphoreType.DMA((4 * CHUNKS + 1,)),
+            pltpu.SemaphoreType.DMA((4 * CHUNKS + 1,)),
             pltpu.SemaphoreType.DMA((len(STREAMS), 6)),
             pltpu.SemaphoreType.DMA((len(STREAMS), 6)),
         ],

time: 48.7 us -> 45.6 us (0.936)
  Pallas kernels: 42.7 us -> 39.6 us
    pallas_call x1, Pallas kernels: 42.7 us -> 39.6 us  [fused(): pl.pallas_call(kernel, out_shape=(jax.ShapeDtypeStruct((tokens, width), b...]
where the time goes in v3:
time: 45.6 us; the launch traced here: 45.5 us
  Pallas kernels  39.6 us (87%)
  local copies, waits for them, and re-layouts  3.49 us (8%)
  other arithmetic  1.7 us (4%)
  between operations  0.67 us (1%)
    pallas_call x1, Pallas kernels, fused(): pl.pallas_call(kernel, out_shape=(jax.ShapeDtypeStruct((tokens, width), b...  39.6 us
    unnamed x7, local copies, waits for them, and re-layouts  3.2 us
    convert_element_type x1, other arithmetic, dequantize(): (codes.astype(jnp.float32) * scales).astype(jnp.bfloat16).reshape(-1, width)  1.7 us

profile of v3, /device:TPU:0, one launch (start us, length us, event | category | flops | bytes accessed | tf_op | source)
XLA Modules:
  0.0 45.5 jit_solution(419774035456445736)
XLA Ops:
  0.6 1.7 %multiply_convert_fusion = bf16[256,4,512]{2,1,0:T(4,128)(2,1)S(1)} fusion(bf16[256,4,512]{2,1,0:T(4,128)(2,1)} %param.6, f32[256]{0:T(256)} %bitcast.1), kind=kLoop, calls=%fused_computation | loop fusion | flops 1572864 | bytes 2098176 | tf_op jit(solution)/shard_map/convert_element_type | solution.py:13
  2.3 0.0 copy-start
  2.3 0.0 copy-start.1
  2.4 0.3 reshape_reshape.3.own
  2.7 0.9 %copy-done = bf16[128,4096]{1,0:T(8,128)(2,1)S(1)} copy-done((bf16[128,4096]{1,0:T(8,128)(2,1)S(1)}, bf16[128,4096]{1,0:T(8,128)(2,1)}, u32[]{:S(2)}) %copy-start) | copy-done | bytes 1048600
  3.6 0.0 copy-done.1
  3.6 39.6 %shard_map.67 = (bf16[128,512]{1,0:T(8,128)(2,1)S(1)}, bf16[128,4096]{1,0:T(8,128)(2,1)S(1)}, bf16[128,512]{1,0:T(8,128)(2,1)S(1)}) custom-call(bf16[128,4096]{1,0:T(8,128)(2,1)S(1)} %copy-done, bf16[128,512]{1,0:T(8,128)(2,1)S(1)} %copy-done.1, bf16[2,512,512]{2,1,0:T(8,128)(2,1)S(1)} %reshape_reshape.3.own), custom_call_target="tpu_custom_call" | custom-call | flops 1610612736 | bytes 4194304 | tf_op jit(solution)/shard_map/pallas_call | solution.py:271
  43.2 0.7 %copy.10 = bf16[128,512]{1,0:T(8,128)(2,1)} copy(bf16[128,512]{1,0:T(8,128)(2,1)S(1)} %get-tuple-element.6) | data formatting | bytes 262144
  43.8 1.0 %copy.11 = bf16[128,4096]{1,0:T(8,128)(2,1)} copy(bf16[128,4096]{1,0:T(8,128)(2,1)S(1)} %get-tuple-element.7) | data formatting | bytes 2097152
  44.8 0.7 %copy.12 = bf16[128,512]{1,0:T(8,128)(2,1)} copy(bf16[128,512]{1,0:T(8,128)(2,1)S(1)} %get-tuple-element.8) | data formatting | bytes 262144
Async XLA Ops:
  2.3 1.2 %copy-start = (bf16[128,4096]{1,0:T(8,128)(2,1)S(1)}, bf16[128,4096]{1,0:T(8,128)(2,1)}, u32[]{:S(2)}) copy-start(bf16[128,4096]{1,0:T(8,128)(2,1)} %feat.1) | copy-start | bytes 3145732
  2.3 1.2 %copy-start.1 = (bf16[128,512]{1,0:T(8,128)(2,1)S(1)}, bf16[128,512]{1,0:T(8,128)(2,1)}, u32[]{:S(2)}) copy-start(bf16[128,512]{1,0:T(8,128)(2,1)} %cot.1) | copy-start | bytes 393220

commit v4 on v3

--- a/solution.py
+++ b/solution.py
@@ -67,6 +67,7 @@
     ("core", "zl", "x", "y", "zh"),
 )
 CHUNKS = 4
+SPLIT = 3
 MESH = pl.DeviceIdType.MESH
 
 
@@ -136,9 +137,15 @@
         for k, h in enumerate((mine, other))
     ]
     streams = range(len(STREAMS))
-    first = [g_copy(s, 5, 0, 24, 8) for s in streams]
+    first = [
+        [g_copy(s, 5 + step, step, 24 >> step, 8 >> step) for step in range(SPLIT)]
+        for s in streams
+    ]
     g = [
-        [g_copy(s, step, step, 16 >> step, 8 if step == 0 else 16 >> step) for step in range(5)]
+        [
+            g_copy(s, step, step, 16 >> step, (8 if step < SPLIT else 16) >> step)
+            for step in range(5)
+        ]
         for s in streams
     ]
 
@@ -175,12 +182,12 @@
 
     for n in range(24, 32):
         partial(n)
-    first[0].start()
-    first[2].start()
+    first[0][0].start()
+    first[2][0].start()
     for n in (18, 19, 22, 23):
         partial(n)
-    first[1].start()
-    first[3].start()
+    first[1][0].start()
+    first[3][0].start()
     for n in (16, 17, 20, 21):
         partial(n)
     for s in streams:
@@ -196,14 +203,18 @@
                 part[s, j].astype(jnp.float32) + got[s, base + j].astype(jnp.float32)
             ).astype(jnp.bfloat16)
 
-    def advance(s, step):
+    def advance_all(step):
         n = 16 >> step
-        (first[s] if step == 0 else g[s][step]).wait_recv()
-        add(s, n // 2, n // 2, n)
-        g[s][step + 1].start()
-        if step == 0:
-            g[s][0].wait_recv()
-        add(s, 0, n // 2, n)
+        for s in streams:
+            (first[s] if step < SPLIT else g[s])[step].wait_recv()
+            add(s, n // 2, n // 2, n)
+            if step + 1 < SPLIT:
+                first[s][step + 1].start()
+            g[s][step + 1].start()
+        for s in streams:
+            if step < SPLIT:
+                g[s][step].wait_recv()
+            add(s, 0, n // 2, n)
 
     def finish(s):
         g[s][4].wait_recv()
@@ -222,10 +233,6 @@
         gin_ref[:, pl.ds(at, half)] = lax.dot_general(
             cot[...], block[...], (((1,), (1,)), ((), ())), preferred_element_type=jnp.float32
         ).astype(jnp.bfloat16)
-
-    def advance_all(step):
-        for s in streams:
-            advance(s, step)
 
     forward(0)
     advance_all(0)
@@ -255,7 +262,7 @@
     key_ref[...] = acc[...].astype(jnp.bfloat16)
     for s in streams:
         finish(s)
-    for copy in (over_core, *over_y, *onward, *core_mine, *core_other, *first, *sum(g, [])):
+    for copy in (over_core, *over_y, *onward, *core_mine, *core_other, *sum(first, []), *sum(g, [])):
         copy.wait_send()
 
 
@@ -284,8 +291,8 @@
             pltpu.VMEM((tokens, width), jnp.float32),
             pltpu.SemaphoreType.DMA((4 * CHUNKS + 1,)),
             pltpu.SemaphoreType.DMA((4 * CHUNKS + 1,)),
-            pltpu.SemaphoreType.DMA((len(STREAMS), 6)),
-            pltpu.SemaphoreType.DMA((len(STREAMS), 6)),
+            pltpu.SemaphoreType.DMA((len(STREAMS), 5 + SPLIT)),
+            pltpu.SemaphoreType.DMA((len(STREAMS), 5 + SPLIT)),
         ],
         compiler_params=pltpu.CompilerParams(
             collective_id=0, has_side_effects=True, vmem_limit_bytes=40 * 1024 * 1024

time: 45.6 us -> 44.7 us (0.980)
  Pallas kernels: 39.6 us -> 38.7 us
    pallas_call x1, Pallas kernels: 39.6 us -> 38.7 us  [fused(): pl.pallas_call(kernel, out_shape=(jax.ShapeDtypeStruct((tokens, width), b...]
where the time goes in v4:
time: 44.7 us; the launch traced here: 44.5 us
  Pallas kernels  38.7 us (87%)
  local copies, waits for them, and re-layouts  3.49 us (8%)
  other arithmetic  1.7 us (4%)
  between operations  0.67 us (1%)
    pallas_call x1, Pallas kernels, fused(): pl.pallas_call(kernel, out_shape=(jax.ShapeDtypeStruct((tokens, width), b...  38.7 us
    unnamed x7, local copies, waits for them, and re-layouts  3.2 us
    convert_element_type x1, other arithmetic, dequantize(): (codes.astype(jnp.float32) * scales).astype(jnp.bfloat16).reshape(-1, width)  1.7 us

profile of v4, /device:TPU:0, one launch (start us, length us, event | category | flops | bytes accessed | tf_op | source)
XLA Modules:
  0.0 44.5 jit_solution(4013805815214080554)
XLA Ops:
  0.6 1.7 %multiply_convert_fusion = bf16[256,4,512]{2,1,0:T(4,128)(2,1)S(1)} fusion(bf16[256,4,512]{2,1,0:T(4,128)(2,1)} %param.6, f32[256]{0:T(256)} %bitcast.1), kind=kLoop, calls=%fused_computation | loop fusion | flops 1572864 | bytes 2098176 | tf_op jit(solution)/shard_map/convert_element_type | solution.py:13
  2.3 0.0 copy-start
  2.3 0.0 copy-start.1
  2.4 0.3 reshape_reshape.3.own
  2.7 0.9 %copy-done = bf16[128,4096]{1,0:T(8,128)(2,1)S(1)} copy-done((bf16[128,4096]{1,0:T(8,128)(2,1)S(1)}, bf16[128,4096]{1,0:T(8,128)(2,1)}, u32[]{:S(2)}) %copy-start) | copy-done | bytes 1048600
  3.6 0.0 copy-done.1
  3.6 38.7 %shard_map.67 = (bf16[128,512]{1,0:T(8,128)(2,1)S(1)}, bf16[128,4096]{1,0:T(8,128)(2,1)S(1)}, bf16[128,512]{1,0:T(8,128)(2,1)S(1)}) custom-call(bf16[128,4096]{1,0:T(8,128)(2,1)S(1)} %copy-done, bf16[128,512]{1,0:T(8,128)(2,1)S(1)} %copy-done.1, bf16[2,512,512]{2,1,0:T(8,128)(2,1)S(1)} %reshape_reshape.3.own), custom_call_target="tpu_custom_call" | custom-call | flops 1610612736 | bytes 4194304 | tf_op jit(solution)/shard_map/pallas_call | solution.py:278
  42.2 0.7 %copy.10 = bf16[128,512]{1,0:T(8,128)(2,1)} copy(bf16[128,512]{1,0:T(8,128)(2,1)S(1)} %get-tuple-element.6) | data formatting | bytes 262144
  42.9 1.0 %copy.11 = bf16[128,4096]{1,0:T(8,128)(2,1)} copy(bf16[128,4096]{1,0:T(8,128)(2,1)S(1)} %get-tuple-element.7) | data formatting | bytes 2097152
  43.9 0.7 %copy.12 = bf16[128,512]{1,0:T(8,128)(2,1)} copy(bf16[128,512]{1,0:T(8,128)(2,1)S(1)} %get-tuple-element.8) | data formatting | bytes 262144
Async XLA Ops:
  2.3 1.2 %copy-start = (bf16[128,4096]{1,0:T(8,128)(2,1)S(1)}, bf16[128,4096]{1,0:T(8,128)(2,1)}, u32[]{:S(2)}) copy-start(bf16[128,4096]{1,0:T(8,128)(2,1)} %feat.1) | copy-start | bytes 3145732
  2.3 1.2 %copy-start.1 = (bf16[128,512]{1,0:T(8,128)(2,1)S(1)}, bf16[128,512]{1,0:T(8,128)(2,1)}, u32[]{:S(2)}) copy-start(bf16[128,512]{1,0:T(8,128)(2,1)} %cot.1) | copy-start | bytes 393220

commit v5 on v4

--- a/solution.py
+++ b/solution.py
@@ -64,7 +64,7 @@
     ("core", "x", "y", "zl", "zh"),
     ("core", "zl", "y", "x", "zh"),
     ("core", "x", "zl", "y", "zh"),
-    ("core", "zl", "x", "y", "zh"),
+    ("core", "y", "zl", "x", "zh"),
 )
 CHUNKS = 4
 SPLIT = 3
@@ -184,11 +184,13 @@
         partial(n)
     first[0][0].start()
     first[2][0].start()
-    for n in (18, 19, 22, 23):
+    for n in range(20, 24):
+        partial(n)
+    first[3][0].start()
+    for n in (18, 19):
         partial(n)
     first[1][0].start()
-    first[3][0].start()
-    for n in (16, 17, 20, 21):
+    for n in (16, 17):
         partial(n)
     for s in streams:
         g[s][0].start()

time: 44.7 us -> 44 us (0.984)
  Pallas kernels: 38.7 us -> 37.9 us
    pallas_call x1, Pallas kernels: 38.7 us -> 37.9 us  [fused(): pl.pallas_call(kernel, out_shape=(jax.ShapeDtypeStruct((tokens, width), b...]
where the time goes in v5:
time: 44 us; the launch traced here: 43.8 us
  Pallas kernels  37.9 us (86%)
  local copies, waits for them, and re-layouts  3.49 us (8%)
  other arithmetic  1.7 us (4%)
  between operations  0.67 us (2%)
    pallas_call x1, Pallas kernels, fused(): pl.pallas_call(kernel, out_shape=(jax.ShapeDtypeStruct((tokens, width), b...  37.9 us
    unnamed x7, local copies, waits for them, and re-layouts  3.2 us
    convert_element_type x1, other arithmetic, dequantize(): (codes.astype(jnp.float32) * scales).astype(jnp.bfloat16).reshape(-1, width)  1.7 us

profile of v5, /device:TPU:0, one launch (start us, length us, event | category | flops | bytes accessed | tf_op | source)
XLA Modules:
  0.0 43.8 jit_solution(14214437940098164160)
XLA Ops:
  0.6 1.7 %multiply_convert_fusion = bf16[256,4,512]{2,1,0:T(4,128)(2,1)S(1)} fusion(bf16[256,4,512]{2,1,0:T(4,128)(2,1)} %param.6, f32[256]{0:T(256)} %bitcast.1), kind=kLoop, calls=%fused_computation | loop fusion | flops 1572864 | bytes 2098176 | tf_op jit(solution)/shard_map/convert_element_type | solution.py:13
  2.3 0.0 copy-start
  2.3 0.0 copy-start.1
  2.4 0.3 reshape_reshape.3.own
  2.7 0.9 %copy-done = bf16[128,4096]{1,0:T(8,128)(2,1)S(1)} copy-done((bf16[128,4096]{1,0:T(8,128)(2,1)S(1)}, bf16[128,4096]{1,0:T(8,128)(2,1)}, u32[]{:S(2)}) %copy-start) | copy-done | bytes 1048600
  3.6 0.0 copy-done.1
  3.6 37.9 %shard_map.67 = (bf16[128,512]{1,0:T(8,128)(2,1)S(1)}, bf16[128,4096]{1,0:T(8,128)(2,1)S(1)}, bf16[128,512]{1,0:T(8,128)(2,1)S(1)}) custom-call(bf16[128,4096]{1,0:T(8,128)(2,1)S(1)} %copy-done, bf16[128,512]{1,0:T(8,128)(2,1)S(1)} %copy-done.1, bf16[2,512,512]{2,1,0:T(8,128)(2,1)S(1)} %reshape_reshape.3.own), custom_call_target="tpu_custom_call" | custom-call | flops 1610612736 | bytes 4194304 | tf_op jit(solution)/shard_map/pallas_call | solution.py:280
  41.5 0.7 %copy.10 = bf16[128,512]{1,0:T(8,128)(2,1)} copy(bf16[128,512]{1,0:T(8,128)(2,1)S(1)} %get-tuple-element.6) | data formatting | bytes 262144
  42.2 1.0 %copy.11 = bf16[128,4096]{1,0:T(8,128)(2,1)} copy(bf16[128,4096]{1,0:T(8,128)(2,1)S(1)} %get-tuple-element.7) | data formatting | bytes 2097152
  43.2 0.7 %copy.12 = bf16[128,512]{1,0:T(8,128)(2,1)} copy(bf16[128,512]{1,0:T(8,128)(2,1)S(1)} %get-tuple-element.8) | data formatting | bytes 262144
Async XLA Ops:
  2.3 1.2 %copy-start = (bf16[128,4096]{1,0:T(8,128)(2,1)S(1)}, bf16[128,4096]{1,0:T(8,128)(2,1)}, u32[]{:S(2)}) copy-start(bf16[128,4096]{1,0:T(8,128)(2,1)} %feat.1) | copy-start | bytes 3145732
  2.3 1.2 %copy-start.1 = (bf16[128,512]{1,0:T(8,128)(2,1)S(1)}, bf16[128,512]{1,0:T(8,128)(2,1)}, u32[]{:S(2)}) copy-start(bf16[128,512]{1,0:T(8,128)(2,1)} %cot.1) | copy-start | bytes 393220
